TPU v7x, 32 devices: a whole 2x2x4 slice. The times are simulated.
32 devices in a mesh: gx: 4 (over y, core), gy: 8 (over z, x).
Axes of the slice: x: 2, y: 2, z: 4, core: 2. Of those that a mesh axis runs over, the one named last changes fastest.
Arguments:
- model_state: float32 [200, 128, 1024], P(None, 'gx', 'gy'), may hold values from -6 to 6
- obs_cell: int32 [32, 2048], P(('gx', 'gy')), may hold values from 0 to 4095
- obs_count: int32 [32, 32], P(('gx', 'gy')), may hold values from 0 to 64, as said below
- obs_value: float32 [16, 65536], P(None, ('gx', 'gy')), may hold values from -6 to 6
- obs_weight: float32 [16, 65536], P(None, ('gx', 'gy')), may hold values from 0.25 to 4
- predictor: float32 [8, 65536], P(None, ('gx', 'gy')), may hold values from -6 to 6
- bias_coef: float32 [16, 8], replicated, may hold values from -3 to 3
- weight_in: float32 [768, 200], replicated, may hold values from -0.4375 to 0.4375
- bias_in: float32 [768], replicated, may hold values from -3 to 3
- weight_mid: float32 [768, 768], replicated, may hold values from -0.21875 to 0.21875
- bias_mid: float32 [768], replicated, may hold values from -3 to 3
- weight_out: float32 [16, 768], replicated, may hold values from -0.21875 to 0.21875
- bias_out: float32 [16], replicated, may hold values from -4 to 4
Outputs:
- gradient: float32 [200, 128, 1024], P(None, 'gx', 'gy')
- evolved: float32 [16, 65536], P(None, ('gx', 'gy'))
- bias_gradient: float32 [16, 8], replicated
Inputs may be any that keep to these rules, and one draw needn't show every extreme that they name: obs_count[o, s] is how many of the 64 slots that owner o keeps for grid block s are used, from the first on; for some block s every owner uses all 64. `obs_cell`: a cell within a block is numbered row within the block times 128 plus column within the block.
All inputs are finite; a program needn't handle non-finite values.
Results may differ from a plain program's by a relative error of at most 0.000096.
Values sent between devices are 32-bit elements; how exact they have to be, the bound alone decides.
A program may use at most 64 MiB of HBM per device.

v0:
```python
import jax
import jax.numpy as jnp
from jax import lax
from jax.sharding import PartitionSpec as P


def product(lhs_array, rhs_array):
    return jnp.dot(
        lhs_array, rhs_array, preferred_element_type=jnp.float32, precision=lax.Precision.HIGHEST
    )


def observe(
    profile,
    obs_rows,
    weight_rows,
    pred_rows,
    bias_coef,
    weight_in,
    bias_in,
    weight_mid,
    bias_mid,
    weight_out,
    bias_out,
):
    hidden_in = jnp.tanh(product(weight_in, profile) + bias_in[:, None])
    hidden_mid = jnp.tanh(product(weight_mid, hidden_in) + bias_mid[:, None])
    model_out = product(weight_out, hidden_mid) + bias_out[:, None] + product(bias_coef, pred_rows)
    residual_term = weight_rows * (model_out - obs_rows)
    back_mid = product(weight_out.T, residual_term) * (1.0 - hidden_mid * hidden_mid)
    back_in = product(weight_mid.T, back_mid) * (1.0 - hidden_in * hidden_in)
    increment = product(weight_in.T, back_in)
    bias_part = product(residual_term, pred_rows.T)
    return (model_out, increment, bias_part)


def exchange_blocks(block_data):
    return lax.all_to_all(block_data, ("gx", "gy"), split_axis=1, concat_axis=1, tiled=True)


def per_device(
    model_state,
    obs_cell,
    obs_count,
    obs_value,
    obs_weight,
    predictor,
    bias_coef,
    weight_in,
    bias_in,
    weight_mid,
    bias_mid,
    weight_out,
    bias_out,
):
    groups_x = lax.axis_size("gx")
    devices = groups_x * lax.axis_size("gy")
    features, block_rows, block_cols = model_state.shape
    slot_total = obs_cell.shape[1]
    capacity = slot_total // devices
    asked_cells = lax.all_to_all(obs_cell, ("gx", "gy"), split_axis=1, concat_axis=1, tiled=True)[0]
    columns = jnp.take(model_state.reshape(features, block_rows * block_cols), asked_cells, axis=1)
    valid_slot = (jnp.arange(capacity, dtype=jnp.int32)[None, :] < obs_count[0][:, None]).reshape(
        slot_total
    )
    masked_weight = jnp.where(valid_slot[None, :], obs_weight, jnp.float32(0.0))
    channels = obs_value.shape[0]
    outgoing = jnp.concatenate([obs_value, masked_weight, predictor], axis=0)
    incoming = exchange_blocks(outgoing)
    local_out, returned, bias_part = observe(
        columns,
        incoming[:channels],
        incoming[channels : 2 * channels],
        incoming[2 * channels :],
        bias_coef,
        weight_in,
        bias_in,
        weight_mid,
        bias_mid,
        weight_out,
        bias_out,
    )
    model_out = exchange_blocks(local_out)
    gradient = (
        jnp.zeros((features, block_rows * block_cols), jnp.float32).at[:, asked_cells].add(returned)
    )
    bias_gradient = lax.psum(bias_part, ("gx", "gy"))
    evolved = jnp.where(valid_slot[None, :], model_out, jnp.float32(0.0))
    return (gradient.reshape(features, block_rows, block_cols), evolved, bias_gradient)


def solution(mesh):
    in_specs = (
        P(None, "gx", "gy"),
        P(("gx", "gy"), None),
        P(("gx", "gy"), None),
        P(None, ("gx", "gy")),
        P(None, ("gx", "gy")),
        P(None, ("gx", "gy")),
        P(),
        P(),
        P(),
        P(),
        P(),
        P(),
        P(),
    )
    out_specs = (P(None, "gx", "gy"), P(None, ("gx", "gy")), P())
    return jax.shard_map(
        per_device, mesh=mesh, in_specs=in_specs, out_specs=out_specs, check_vma=False
    )
```

profile of v0, /device:TPU:0, one launch (start us, length us, event | category | flops | bytes accessed | tf_op | source)
XLA Modules:
  0.0 180.8 jit_solution(10002537874206958980)
XLA Ops:
  0.6 0.5 broadcast.72
  1.2 1.6 reduce.8
  2.7 0.7 all_to_all.20
  3.4 7.3 %all-to-all-start = ((s32[1,32,64]{2,0,1:T(1,128)}), s32[1,32,64]{2,0,1:T(1,128)S(1)}, u32[]{:S(2)}, u32[]{:S(2)}) async-start(s32[1,32,64]{2,0,1:T(1,128)} %all_to_all.20), calls=%async_computation | async-start | bytes 32768 | tf_op jit(solution)/shard_map/all_to_all | solution.py:61
  10.7 0.7 iota_compare_fusion
  11.5 0.9 broadcast_select_fusion.1
  12.4 1.0 pad_maximum_fusion
  13.7 1.2 copy.37
  14.9 2.2 %reshape.114 = f32[32,1,2560]{2,1,0:T(1,128)} reshape(f32[32,40,64]{2,1,0:T(8,128)} %bitcast.29) | data formatting | bytes 655360
  17.1 5.0 %copy.27 = f32[200,32,128]{0,2,1:T(8,128)} copy(f32[200,32,128]{2,1,0:T(8,128)} %param.13) | data formatting | bytes 6553600 | tf_op args[0]
  22.2 5.8 %all-to-all-start.1 = ((f32[32,1,2560]{2,1,0:T(1,128)}), f32[32,1,2560]{2,1,0:T(1,128)S(1)}, u32[]{:S(2)}, u32[]{:S(2)}) async-start(f32[32,1,2560]{2,1,0:T(1,128)} %reshape.114), calls=%async_computation.1 | async-start | bytes 655360 | tf_op jit(solution)/shard_map/all_to_all | solution.py:38
  28.1 0.7 reduce.9
  28.9 11.0 %gather_fusion = f32[2048,200]{1,0:T(8,128)} fusion(f32[200,4096]{0,1:T(8,128)} %bitcast.25, s32[2048]{0:T(1024)S(1)} %broadcast_clamp_fusion), kind=kCustom, calls=%fused_computation | custom fusion | bytes 3284992 | tf_op jit(solution)/shard_map/jit(_take)/gather | solution.py:62
  39.9 7.5 %fusion.18 = f32[2048,768]{1,0:T(8,128)S(1)} fusion(f32[768,200]{0,1:T(8,128)S(1)} %copy-done.3, f32[2048,200]{1,0:T(8,128)} %gather_fusion, pred[2048]{0:T(1024)(128)(4,1)S(1)} %compare_and_fusion), kind=kOutput, calls=%fused_computation.23 | convolution fusion | flops 3775283200 | bytes 8546304 | tf_op jit(solution)/shard_map/dot_general | solution.py:8
  47.5 17.7 %fusion.8 = f32[2048,768]{1,0:T(8,128)S(1)} fusion(f32[768,768]{1,0:T(8,128)S(1)} %copy-done, f32[2048,768]{1,0:T(8,128)S(1)} %fusion.18, f32[768]{0:T(1024)S(1)} %copy-done.7), kind=kOutput, calls=%fused_computation.12 | convolution fusion | flops 14497087488 | bytes 14945280 | tf_op jit(solution)/shard_map/dot_general | solution.py:8
  65.3 2.6 %copy-done.2 = f32[2048,768]{1,0:T(8,128)} copy-done((f32[2048,768]{1,0:T(8,128)}, f32[2048,768]{1,0:T(8,128)S(1)}, u32[]{:S(2)}) %copy-start.2) | copy-done | bytes 6291480
  67.9 5.9 %fusion.17 = f32[2048,16]{0,1:T(8,128)S(1)} fusion(f32[16,768]{1,0:T(8,128)S(1)} %copy-done.5, f32[2048,768]{1,0:T(8,128)S(1)} %fusion.8, f32[768]{0:T(1024)S(1)} %copy-done.6, f32[16]{0:T(128)S(1)} %copy-done.9), kind=kOutput, calls=%fused_computation.22 | convolution fusion | flops 303595520 | bytes 6474816 | tf_op jit(solution)/shard_map/dot_general | solution.py:8
  73.8 0.5 broadcast.74
  74.4 2.2 %reduce.10 = f32[32,2560]{1,0:T(8,128)} reduce(f32[32,1,2560]{2,1,0:T(1,128)S(1)} %all-to-all-done.1, f32[]{:T(128)} %broadcast.74), dimensions={1}, to_apply=%all_to_all.23.reduce_sub_computation | reduce | bytes 655364 | tf_op jit(solution)/shard_map/all_to_all | solution.py:38
  76.6 1.1 reshape.115
  77.7 0.7 slice.27
  78.6 0.9 copy.28
  80.4 0.8 reshape.116
  81.3 5.8 %all-to-all-start.2 = ((f32[32,1,1024]{2,1,0:T(1,128)}), f32[32,1,1024]{2,1,0:T(1,128)S(1)}, u32[]{:S(2)}, u32[]{:S(2)}) async-start(f32[32,1,1024]{2,1,0:T(1,128)} %reshape.116), calls=%async_computation.2 | async-start | bytes 262144 | tf_op jit(solution)/shard_map/all_to_all | solution.py:38
  87.1 5.4 %fusion.28 = f32[2048,768]{1,0:T(8,128)S(1)} fusion(f32[16,768]{1,0:T(8,128)S(1)} %copy-done.5, f32[16,2048]{1,0:T(8,128)S(1)} %slice.19, f32[16,2048]{1,0:T(8,128)S(1)} %fusion.16, f32[16,2048]{1,0:T(8,128)S(1)} %slice.23), kind=kOutput, calls=%fused_computation.42 | convolution fusion | flops 302055424 | bytes 6733824 | tf_op jit(solution)/shard_map/dot_general | solution.py:8
  92.5 19.0 %fusion.2 = f32[2048,768]{1,0:T(8,128)S(1)} fusion(f32[768,768]{1,0:T(8,128)S(1)} %copy-done, f32[2048,768]{1,0:T(8,128)S(1)} %fusion.28, f32[2048,768]{1,0:T(8,128)} %copy-done.2, f32[768]{0:T(1024)S(1)} %copy-done.6), kind=kOutput, calls=%fused_computation.4 | convolution fusion | flops 14501806080 | bytes 21236736 | tf_op jit(solution)/shard_map/dot_general | solution.py:8
  111.6 7.1 %fusion = f32[2048,200]{1,0:T(8,128)} fusion(f32[768,200]{0,1:T(8,128)S(1)} %copy-done.4, f32[2048,768]{1,0:T(8,128)S(1)} %fusion.2, f32[2048,768]{1,0:T(8,128)S(1)} %bitcast.27, f32[768]{0:T(1024)S(1)} %copy-done.7), kind=kOutput, calls=%fused_computation.2 | convolution fusion | flops 3781165056 | bytes 14838784 | tf_op jit(solution)/shard_map/dot_general | solution.py:8
  118.7 14.1 %scatter_custom_fusion = f32[200,4096]{0,1:T(8,128)} fusion(s32[2048]{0:T(1024)S(1)} %bitcast.36, f32[2048,200]{1,0:T(8,128)} %fusion, f32[]{:T(128)} %constant.6.clone.1), kind=kCustom, calls=%fused_computation.25 | custom fusion | flops 409600 | bytes 3277312 | tf_op jit(solution)/shard_map/scatter-add | solution.py:85
  132.8 5.0 %copy.33 = f32[200,32,128]{2,1,0:T(8,128)} copy(f32[200,32,128]{0,2,1:T(8,128)} %bitcast.28) | data formatting | bytes 6553600
  138.0 40.6 %psum.7 = f32[16,8]{0,1:T(8,128)} all-reduce(f32[16,8]{0,1:T(8,128)S(1)} %fusion.27), channel_id=1, replica_groups=mesh['gx'=4,'gy'=8] {'gx','gy'}, use_global_device_ids=true, to_apply=%region_1.2 | all-reduce | flops 128 | bytes 1024 | tf_op jit(solution)/shard_map/psum | solution.py:87
  178.6 0.9 reduce.11
  179.9 0.7 broadcast_select_fusion
  (47 shorter events, 2.2 us)
Async XLA Ops:
  0.6 46.9 %copy-start = (f32[768,768]{1,0:T(8,128)S(1)}, f32[768,768]{1,0:T(8,128)}, u32[]{:S(2)}) copy-start(f32[768,768]{1,0:T(8,128)} %param.22) | copy-start | bytes 7077892
  3.4 18.8 %all-to-all-start = ((s32[1,32,64]{2,0,1:T(1,128)}), s32[1,32,64]{2,0,1:T(1,128)S(1)}, u32[]{:S(2)}, u32[]{:S(2)}) async-start(s32[1,32,64]{2,0,1:T(1,128)} %all_to_all.20), calls=%async_computation | async-start | bytes 32768 | tf_op jit(solution)/shard_map/all_to_all | solution.py:61
  22.2 51.7 %all-to-all-start.1 = ((f32[32,1,2560]{2,1,0:T(1,128)}), f32[32,1,2560]{2,1,0:T(1,128)S(1)}, u32[]{:S(2)}, u32[]{:S(2)}) async-start(f32[32,1,2560]{2,1,0:T(1,128)} %reshape.114), calls=%async_computation.1 | async-start | bytes 655360 | tf_op jit(solution)/shard_map/all_to_all | solution.py:38
  28.9 11.0 %copy-start.3 = (f32[768,200]{0,1:T(8,128)S(1)}, f32[768,200]{0,1:T(8,128)}, u32[]{:S(2)}) copy-start(f32[768,200]{0,1:T(8,128)} %param.20) | copy-start | bytes 1843204
  39.9 7.6 %copy-start.7 = (f32[768]{0:T(1024)S(1)}, f32[768]{0:T(1024)}, u32[]{:S(2)}) copy-start(f32[768]{0:T(1024)} %param.21) | copy-start | bytes 9220
  47.5 17.7 %copy-start.1 = (f32[2048,768]{1,0:T(8,128)}, f32[2048,768]{1,0:T(8,128)S(1)}, u32[]{:S(2)}) copy-start(f32[2048,768]{1,0:T(8,128)S(1)} %fusion.18) | copy-start | bytes 18874372
  47.5 20.4 %copy-start.5 = (f32[16,768]{1,0:T(8,128)S(1)}, f32[16,768]{1,0:T(8,128)}, u32[]{:S(2)}) copy-start(f32[16,768]{1,0:T(8,128)} %param.24) | copy-start | bytes 147460
  47.5 20.4 %copy-start.6 = (f32[768]{0:T(1024)S(1)}, f32[768]{0:T(1024)}, u32[]{:S(2)}) copy-start(f32[768]{0:T(1024)} %param.23) | copy-start | bytes 9220
  47.5 20.4 %copy-start.9 = (f32[16]{0:T(128)S(1)}, f32[16]{0:T(128)}, u32[]{:S(2)}) copy-start(f32[16]{0:T(128)} %param.25) | copy-start | bytes 196
  65.2 2.7 %copy-start.2 = (f32[2048,768]{1,0:T(8,128)}, f32[2048,768]{1,0:T(8,128)S(1)}, u32[]{:S(2)}) copy-start(f32[2048,768]{1,0:T(8,128)S(1)} %fusion.8) | copy-start | bytes 18874372
  67.9 11.9 %copy-start.8 = (f32[16,8]{0,1:T(8,128)S(1)}, f32[16,8]{0,1:T(8,128)}, u32[]{:S(2)}) copy-start(f32[16,8]{0,1:T(8,128)} %param.19) | copy-start | bytes 1540
  81.3 97.3 %all-to-all-start.2 = ((f32[32,1,1024]{2,1,0:T(1,128)}), f32[32,1,1024]{2,1,0:T(1,128)S(1)}, u32[]{:S(2)}, u32[]{:S(2)}) async-start(f32[32,1,1024]{2,1,0:T(1,128)} %reshape.116), calls=%async_computation.2 | async-start | bytes 262144 | tf_op jit(solution)/shard_map/all_to_all | solution.py:38
  87.1 24.4 %slice-start = ((s8[6291456]{0:T(1024)(128)(4,1)}), s8[4194304]{0:T(1024)(128)(4,1)S(1)}, s32[]{:S(2)}) async-start(s8[6291456]{0:T(1024)(128)(4,1)} %bitcast.26), calls=%async_computation.3 | async-start | bytes 8388608
  92.5 19.0 %slice-start.1 = ((s8[6291456]{0:T(1024)(128)(4,1)}), s8[2097152]{0:T(1024)(128)(4,1)S(1)}, s32[]{:S(2)}) async-start(s8[6291456]{0:T(1024)(128)(4,1)} %bitcast.26), calls=%async_computation.4 | async-start | bytes 4194304
  92.5 19.0 %copy-start.4 = (f32[768,200]{0,1:T(8,128)S(1)}, f32[768,200]{0,1:T(8,128)}, u32[]{:S(2)}) copy-start(f32[768,200]{0,1:T(8,128)} %param.20) | copy-start | bytes 1843204
where the time goes:
time: 184 us; the launch traced here: 181 us
  matrix products  63.1 us (34%)
  blocking collectives  40.6 us (22%)
  local copies, waits for them, and re-layouts  34.1 us (19%)
  other arithmetic  22.8 us (12%)
  starting transfers between devices  19 us (10%)
    dot_general x8, matrix products, product(): jnp.dot(lhs_array, rhs_array, preferred_element_type=jnp.float32, precisi...  63.1 us
    psum x1, blocking collectives, per_device(): bias_gradient = lax.psum(bias_part, ('gx', 'gy'))  40.6 us
    unnamed x31, local copies, waits for them, and re-layouts  17.6 us
    scatter-add x1, other arithmetic, per_device(): jnp.zeros((features, block_rows * block_cols), jnp.float32)  14.1 us
    all_to_all x2, starting transfers between devices, exchange_blocks(): lax.all_to_all(block_data, ('gx', 'gy'), split_axis=1, concat_axis=1, til...  11.7 us
    gather x1, local copies, waits for them, and re-layouts, per_device(): jnp.take(model_state.reshape(features, block_rows * block_cols), asked_ce...  11 us
    all_to_all x1, starting transfers between devices, per_device(): lax.all_to_all(obs_cell, ('gx', 'gy'), split_axis=1, concat_axis=1, tiled...  7.3 us
  transfers between devices with their start and end apart: 3, of which 0 were waited for; matrix products, arithmetic and copies ran while one was open for 58% of the time, Pallas kernels for 0%

commit v1 on v0

v1 whole, which is shorter than its diff:
```python
import functools

import jax
import jax.numpy as jnp
from jax import lax
from jax.experimental import pallas as pl
from jax.experimental.pallas import tpu as pltpu
from jax.sharding import PartitionSpec as P

BF = jnp.bfloat16
F32 = jnp.float32


def round_up(value, step):
    return (value + step - 1) // step * step


def split_parts(x):
    hi = x.astype(BF)
    lo = (x - hi.astype(F32)).astype(BF)
    return hi, lo


def dot(a, b):
    return jnp.dot(a, b, preferred_element_type=F32)


def store_cat(ref, x, step):
    rows = x.shape[0]
    hi, lo = split_parts(x)
    ref[0:rows, :] = hi
    ref[step : step + rows, :] = lo
    ref[2 * step : 2 * step + rows, :] = hi


def weight_cat(ref, w, step):
    cols = w.shape[1]
    hi, lo = split_parts(w)
    ref[:, 0:cols] = hi
    ref[:, step : step + cols] = hi
    ref[:, 2 * step : 2 * step + cols] = lo


def prepare(w1t_ref, w2_ref, wo_ref, w1c, w1tc, w2c, w2tc, woc, wotc, pcat, rcat, padded, feat_pad):
    features, hid = w1t_ref.shape
    channels = wo_ref.shape[0]
    kp = padded.shape[0]
    padded[...] = jnp.zeros_like(padded)
    padded[0:features, :] = w1t_ref[...]
    weight_cat(w1tc, padded[0:feat_pad, :], hid)
    weight_cat(w1c, padded[...].T, kp)
    w2 = w2_ref[...]
    weight_cat(w2c, w2, hid)
    weight_cat(w2tc, w2.T, hid)
    wo = wo_ref[...]
    weight_cat(woc, wo, hid)
    hi = wo.astype(BF).astype(F32)
    padded[...] = jnp.zeros_like(padded)
    padded[0:channels, :] = hi
    padded[channels : 2 * channels, :] = hi
    padded[2 * channels : 3 * channels, :] = wo - hi
    wotc[...] = padded[0:128, :].T.astype(BF)
    pcat[...] = jnp.zeros_like(pcat)
    rcat[...] = jnp.zeros_like(rcat)


def split_state(st_ref, sp, features, feat_pad, block_rows):
    def body(r, carry):
        x = st_ref[pl.ds(r, features, stride=block_rows), :]
        if feat_pad > features:
            x = jnp.concatenate([x, jnp.zeros((feat_pad - features, x.shape[1]), F32)], axis=0)
        hi, lo = split_parts(x)
        at = pl.ds(pl.multiple_of(r * 128, 128), 128)
        sp[0:feat_pad, at] = hi
        sp[feat_pad : 2 * feat_pad, at] = lo
        return carry

    lax.fori_loop(0, block_rows, body, 0)


def build_onehot(cell, oh, at, block_rows, block_cols):
    n = cell.shape[1]
    row = jnp.floor(cell * (1.0 / block_cols))
    col = cell - row * block_cols
    lanes = lax.broadcasted_iota(jnp.int32, (block_cols, n), 0).astype(F32)
    colhot = jnp.where(lanes == col, 1.0, 0.0).astype(BF).reshape(block_cols // 16, 16, n)
    for r in range(block_rows):
        hit = jnp.broadcast_to(jnp.where(row == float(r), 1.0, 0.0), (16, n)).astype(BF)
        oh[r * block_cols : (r + 1) * block_cols, at] = (colhot * hit[None]).reshape(block_cols, n)


def compute_kernel(
    dims, in_ref, coef_ref, st_ref, w1t_ref, b1_ref, w2_ref, b2_ref, wo_ref, bo_ref,
    grad_ref, out_ref, bias_ref,
    w1c, w1tc, w2c, w2tc, woc, wotc, sp, oh, pcat, hcat, rcat, h1, h2, inc, res, padded,
):
    features, block_rows, block_cols, ts = dims
    hid = w2_ref.shape[0]
    channels = wo_ref.shape[0]
    preds = coef_ref.shape[1]
    feat_pad = sp.shape[0] // 2
    kp = padded.shape[0]
    slots = in_ref.shape[1]
    prepare(w1t_ref, w2_ref, wo_ref, w1c, w1tc, w2c, w2tc, woc, wotc, pcat, rcat, padded, feat_pad)
    split_state(st_ref, sp, features, feat_pad, block_rows)

    def chunk(t, carry):
        at = pl.ds(pl.multiple_of(t * ts, 128), ts)
        obs = in_ref[0:channels, at]
        wgt = in_ref[channels : 2 * channels, at]
        pred = in_ref[2 * channels : 2 * channels + preds, at]
        cell = in_ref[2 * channels + preds : 2 * channels + preds + 1, at]
        build_onehot(cell, oh, at, block_rows, block_cols)
        picked = dot(sp[...], oh[:, at]).astype(BF)
        pcat[0:feat_pad, :] = picked[0:feat_pad]
        pcat[kp : kp + feat_pad, :] = picked[feat_pad:]
        pcat[2 * kp : 2 * kp + feat_pad, :] = picked[0:feat_pad]
        a1 = jnp.tanh(dot(w1c[...], pcat[...]) + b1_ref[...])
        h1[...] = a1
        store_cat(hcat, a1, hid)
        a2 = jnp.tanh(dot(w2c[...], hcat[...]) + b2_ref[...])
        h2[...] = a2
        store_cat(hcat, a2, hid)
        model = dot(woc[...], hcat[...]) + bo_ref[...]
        for p in range(preds):
            model = model + coef_ref[:, p : p + 1] * pred[p : p + 1, :]
        out_ref[:, at] = model
        residual = wgt * (model - obs)
        res[:, at] = residual
        store_cat(rcat, residual, channels)
        a2 = h2[...]
        store_cat(hcat, dot(wotc[...], rcat[...]) * (1.0 - a2 * a2), hid)
        a1 = h1[...]
        store_cat(hcat, dot(w2tc[...], hcat[...]) * (1.0 - a1 * a1), hid)
        hi, lo = split_parts(dot(w1tc[...], hcat[...]))
        inc[0:feat_pad, at] = hi
        inc[feat_pad : 2 * feat_pad, at] = lo
        return carry

    lax.fori_loop(0, slots // ts, chunk, 0)
    bias_ref[...] = lax.dot_general(
        res[...], in_ref[2 * channels : 2 * channels + preds, :], (((1,), (1,)), ((), ())),
        preferred_element_type=F32, precision=lax.Precision.HIGHEST,
    )
    per = max(1, 256 // block_cols)

    def spread(q, carry):
        cells = pl.ds(pl.multiple_of(q * per * block_cols, 128), per * block_cols)
        got = lax.dot_general(
            inc[...], oh[cells, :], (((1,), (1,)), ((), ())), preferred_element_type=F32
        )
        total = got[0:features] + got[feat_pad : feat_pad + features]
        for k in range(per):
            grad_ref[pl.ds(q * per + k, features, stride=block_rows), :] = total[
                :, k * block_cols : (k + 1) * block_cols
            ]
        return carry

    lax.fori_loop(0, block_rows // per, spread, 0)


def run_compute(incoming, model_state, bias_coef, weight_in, bias_in, weight_mid, bias_mid, weight_out, bias_out):
    features, block_rows, block_cols = model_state.shape
    cells = block_rows * block_cols
    hid = weight_mid.shape[0]
    channels, preds = bias_coef.shape
    slots = incoming.shape[1]
    ts = 512
    fp = round_up(features, 16)
    kp = round_up(features, 256)
    vmem = pl.BlockSpec(memory_space=pltpu.VMEM)
    return pl.pallas_call(
        functools.partial(compute_kernel, (features, block_rows, block_cols, ts)),
        out_shape=(
            jax.ShapeDtypeStruct((features * block_rows, block_cols), F32),
            jax.ShapeDtypeStruct((channels, slots), F32),
            jax.ShapeDtypeStruct((channels, preds), F32),
        ),
        in_specs=[vmem] * 9,
        out_specs=(vmem,) * 3,
        scratch_shapes=[
            pltpu.VMEM((hid, 3 * kp), BF),
            pltpu.VMEM((fp, 3 * hid), BF),
            pltpu.VMEM((hid, 3 * hid), BF),
            pltpu.VMEM((hid, 3 * hid), BF),
            pltpu.VMEM((channels, 3 * hid), BF),
            pltpu.VMEM((hid, 128), BF),
            pltpu.VMEM((2 * fp, cells), BF),
            pltpu.VMEM((cells, slots), BF),
            pltpu.VMEM((3 * kp, ts), BF),
            pltpu.VMEM((3 * hid, ts), BF),
            pltpu.VMEM((128, ts), BF),
            pltpu.VMEM((hid, ts), F32),
            pltpu.VMEM((hid, ts), F32),
            pltpu.VMEM((2 * fp, slots), BF),
            pltpu.VMEM((channels, slots), F32),
            pltpu.VMEM((kp, hid), F32),
        ],
        compiler_params=pltpu.CompilerParams(vmem_limit_bytes=60 * 1024 * 1024),
        name="observe_block",
    )(
        incoming, bias_coef, model_state.reshape(features * block_rows, block_cols), weight_in.T,
        bias_in[:, None], weight_mid, bias_mid[:, None], weight_out, bias_out[:, None],
    )


def exchange_blocks(block_data):
    return lax.all_to_all(block_data, ("gx", "gy"), split_axis=1, concat_axis=1, tiled=True)


def per_device(
    model_state, obs_cell, obs_count, obs_value, obs_weight, predictor, bias_coef,
    weight_in, bias_in, weight_mid, bias_mid, weight_out, bias_out,
):
    devices = lax.axis_size("gx") * lax.axis_size("gy")
    slots = obs_cell.shape[1]
    capacity = slots // devices
    channels, preds = bias_coef.shape
    valid_slot = (
        jnp.arange(capacity, dtype=jnp.int32)[None, :] < obs_count[0][:, None]
    ).reshape(slots)
    masked_weight = jnp.where(valid_slot[None, :], obs_weight, jnp.float32(0.0))
    outgoing = jnp.concatenate(
        [obs_value, masked_weight, predictor, obs_cell.astype(F32)], axis=0
    )
    incoming = exchange_blocks(outgoing)
    gradient, local_out, bias_part = run_compute(
        incoming, model_state, bias_coef, weight_in, bias_in, weight_mid, bias_mid, weight_out, bias_out
    )
    back = jnp.concatenate(
        [
            local_out.reshape(channels, devices, capacity).transpose(1, 0, 2).reshape(devices, channels * capacity),
            jnp.broadcast_to(bias_part.reshape(1, channels * preds), (devices, channels * preds)),
        ],
        axis=1,
    )
    got = lax.all_to_all(back, ("gx", "gy"), split_axis=0, concat_axis=0, tiled=True)
    bias_gradient = jnp.sum(got[:, channels * capacity :], axis=0).reshape(channels, preds)
    model_out = (
        got[:, : channels * capacity].reshape(devices, channels, capacity).transpose(1, 0, 2).reshape(channels, slots)
    )
    evolved = jnp.where(valid_slot[None, :], model_out, jnp.float32(0.0))
    return (gradient.reshape(model_state.shape), evolved, bias_gradient)


def solution(mesh):
    split = ("gx", "gy")
    in_specs = (P(None, "gx", "gy"), P(split, None), P(split, None), P(None, split), P(None, split), P(None, split)) + (P(),) * 7
    out_specs = (P(None, "gx", "gy"), P(None, split), P())
    return jax.shard_map(per_device, mesh=mesh, in_specs=in_specs, out_specs=out_specs, check_vma=False)
```

time: 184 us -> 95.8 us (0.52); the launches traced: 181 us -> 95.4 us
  matrix products: 63.1 us -> 0 us
  Pallas kernels: 0 us -> 52.3 us
  blocking collectives: 40.6 us -> 9.91 us
  local copies, waits for them, and re-layouts: 34.1 us -> 10.3 us
  other arithmetic: 22.8 us -> 5.52 us
  starting transfers between devices: 19 us -> 7.3 us
  waiting for transfers between devices: 0.02 us -> 9.32 us
    dot_general x8 -> x0, matrix products: 63.1 us -> none  [product(): jnp.dot(lhs_array, rhs_array, preferred_element_type=jnp.float32, precisi...]
    pallas_call x0 -> x1, Pallas kernels: none -> 52.3 us  [run_compute(): pl.pallas_call(functools.partial(compute_kernel, (features, block_rows, b...]
    psum x1 -> x0, blocking collectives: 40.6 us -> none  [per_device(): bias_gradient = lax.psum(bias_part, ('gx', 'gy'))]
    unnamed x31 -> x13, local copies, waits for them, and re-layouts: 17.6 us -> 2.73 us
    scatter-add x1 -> x0, other arithmetic: 14.1 us -> none  [per_device(): jnp.zeros((features, block_rows * block_cols), jnp.float32)]
    gather x1 -> x0, local copies, waits for them, and re-layouts: 11 us -> none  [per_device(): jnp.take(model_state.reshape(features, block_rows * block_cols), asked_ce...]
    all_to_all x0 -> x1, blocking collectives: none -> 9.91 us  [per_device(): lax.all_to_all(back, ('gx', 'gy'), split_axis=0, concat_axis=0, tiled=True)]
    all_to_all x2 -> x1, waiting for transfers between devices: 0.01 us -> 9.32 us  [exchange_blocks(): lax.all_to_all(block_data, ('gx', 'gy'), split_axis=1, concat_axis=1, til...]
  transfers between devices with their start and end apart: 3 -> 1, of which waited for: 0 -> 1; matrix products, arithmetic and copies ran while one was open for 58% -> 3% of each run, Pallas kernels for 0% -> 0%
where the time goes in v1:
time: 95.8 us; the launch traced here: 95.4 us
  Pallas kernels  52.3 us (55%)
  local copies, waits for them, and re-layouts  10.3 us (11%)
  blocking collectives  9.91 us (10%)
  waiting for transfers between devices  9.32 us (10%)
  starting transfers between devices  7.3 us (8%)
  other arithmetic  5.52 us (6%)
    pallas_call x1, Pallas kernels, run_compute(): pl.pallas_call(functools.partial(compute_kernel, (features, block_rows, b...  52.3 us
    all_to_all x1, blocking collectives, per_device(): lax.all_to_all(back, ('gx', 'gy'), split_axis=0, concat_axis=0, tiled=True)  9.91 us
    all_to_all x1, waiting for transfers between devices, exchange_blocks(): lax.all_to_all(block_data, ('gx', 'gy'), split_axis=1, concat_axis=1, til...  9.32 us
    all_to_all x1, starting transfers between devices, exchange_blocks(): lax.all_to_all(block_data, ('gx', 'gy'), split_axis=1, concat_axis=1, til...  7.3 us
    unnamed x13, local copies, waits for them, and re-layouts  2.73 us
    all_to_all x5, local copies, waits for them, and re-layouts, exchange_blocks(): lax.all_to_all(block_data, ('gx', 'gy'), split_axis=1, concat_axis=1, til...  2.37 us
  transfers between devices with their start and end apart: 1, of which 1 were waited for; matrix products, arithmetic and copies ran while one was open for 3% of the time, Pallas kernels for 0%

profile of v1, /device:TPU:0, one launch (start us, length us, event | category | flops | bytes accessed | tf_op | source)
XLA Modules:
  0.0 95.4 jit_solution(15276889375387219619)
XLA Ops:
  0.7 0.8 iota_compare_fusion
  1.4 0.1 lt.26
  1.5 0.7 convert_element_type.3
  2.2 0.9 broadcast_select_fusion.1
  3.1 1.0 %pad_maximum_fusion = f32[41,2048]{1,0:T(8,128)S(1)} fusion(f32[1,2048]{1,0:T(1,128)S(1)} %convert_element_type.3, f32[8,2048]{1,0:T(8,128)} %param.18, f32[16,2048]{1,0:T(8,128)S(1)} %broadcast_select_fusion.1, f32[16,2048]{1,0:T(8,128)} %param.16), kind=kLoop, calls=%fused_computation | loop fusion | flops 251904 | bytes 671744 | tf_op jit(solution)/shard_map/concatenate | solution.py:223
  4.1 0.2 all_to_all.15
  4.4 0.4 copy.48
  4.8 1.2 %reshape.56 = f32[32,1,2624]{2,1,0:T(1,128)} reshape(f32[32,41,64]{2,1,0:T(8,128)S(1)} %bitcast.19) | data formatting | bytes 671744
  6.0 7.3 %all-to-all-start = ((f32[32,1,2624]{2,1,0:T(1,128)}), f32[32,1,2624]{2,1,0:T(1,128)S(1)}, u32[]{:S(2)}, u32[]{:S(2)}) async-start(f32[32,1,2624]{2,1,0:T(1,128)} %reshape.56), calls=%async_computation | async-start | bytes 688128 | tf_op jit(solution)/shard_map/all_to_all | solution.py:208
  13.3 0.7 copy.34.coef_ref
  13.9 0.7 copy.37.bo_ref
  14.6 0.9 broadcast_in_dim.40.b1_ref
  15.5 0.9 broadcast_in_dim.41.b2_ref
  16.4 9.3 %all-to-all-done = f32[32,1,2624]{2,1,0:T(1,128)S(1)} async-done(((f32[32,1,2624]{2,1,0:T(1,128)}), f32[32,1,2624]{2,1,0:T(1,128)S(1)}, u32[]{:S(2)}, u32[]{:S(2)}) %all-to-all-start) | async-done | bytes 335904 | tf_op jit(solution)/shard_map/all_to_all | solution.py:208
  25.8 0.5 broadcast.6
  26.3 1.5 %reduce = f32[32,2624]{1,0:T(8,128)S(1)} reduce(f32[32,1,2624]{2,1,0:T(1,128)S(1)} %all-to-all-done, f32[]{:T(128)} %broadcast.6), dimensions={1}, to_apply=%all_to_all.16.reduce_sub_computation | reduce | bytes 671748 | tf_op jit(solution)/shard_map/all_to_all | solution.py:208
  27.7 0.2 reshape.57
  27.9 0.2 copy.33
  28.1 1.0 %all_to_all.17.in_ref = f32[41,2048]{1,0:T(8,128)} reshape(f32[41,32,64]{2,1,0:T(8,128)S(1)} %copy.33) | data formatting | bytes 671744 | tf_op jit(solution)/shard_map/all_to_all | solution.py:208
  29.1 52.3 %observe_block.1 = (f32[6400,128]{1,0:T(8,128)}, f32[16,2048]{1,0:T(8,128)}, f32[16,8]{1,0:T(8,128)}) custom-call(f32[41,2048]{1,0:T(8,128)} %all_to_all.17.in_ref, f32[16,8]{1,0:T(8,128)} %copy.34.coef_ref, f32[6400,128]{1,0:T(8,128)} %bitcast.18, f32[200,768]{1,0:T(8,128)} %bitcast.23, f32[768,1]{1,0:T(8,128)} %broadcast_in_dim.40.b1_ref, ...), custom_call_target="tpu_custom_call" | custom-call | tf_op jit(solution)/shard_map/observe_block/pallas_call | solution.py:172
  81.4 0.8 reshape.55
  82.2 1.0 %reshape.50 = f32[16,32,64]{2,1,0:T(8,128)S(1)} reshape(f32[16,2048]{1,0:T(8,128)} %get-tuple-element.7) | data formatting | bytes 262144 | tf_op jit(solution)/shard_map/reshape | solution.py:232
  83.2 0.2 copy.46
  83.4 0.1 reshape.51
  83.5 0.2 copy.39
  83.7 9.9 %all_to_all.23 = f32[32,1,1152]{2,1,0:T(1,128)S(1)} all-to-all(f32[32,1,1152]{2,1,0:T(1,128)S(1)} %copy.39), channel_id=1, replica_groups=mesh['gx'=4,'gy'=8] {'gx','gy'}, dimensions={0} | all-to-all | bytes 294912 | tf_op jit(solution)/shard_map/all_to_all | solution.py:237
  93.6 0.1 reshape.54
  93.7 0.7 copy.41
  94.4 0.1 reshape.52
  94.5 0.1 copy.40
  94.6 0.1 reshape.53
  94.7 0.7 broadcast_select_fusion
  (13 shorter events, 0.1 us)
Async XLA Ops:
  0.6 12.6 %copy-start.2 = (f32[16,8]{0,1:T(8,128)S(1)}, f32[16,8]{0,1:T(8,128)}, u32[]{:S(2)}) copy-start(f32[16,8]{0,1:T(8,128)} %param.19) | copy-start | bytes 1540
  0.6 13.3 %copy-start.3 = (f32[16]{0:T(128)S(1)}, f32[16]{0:T(128)}, u32[]{:S(2)}) copy-start(f32[16]{0:T(128)} %param.25) | copy-start | bytes 196
  0.7 14.0 %copy-start = (f32[768]{0:T(1024)S(1)}, f32[768]{0:T(1024)}, u32[]{:S(2)}) copy-start(f32[768]{0:T(1024)} %param.21) | copy-start | bytes 9220
  0.7 14.9 %copy-start.1 = (f32[768]{0:T(1024)S(1)}, f32[768]{0:T(1024)}, u32[]{:S(2)}) copy-start(f32[768]{0:T(1024)} %param.23) | copy-start | bytes 9220
  6.0 19.8 %all-to-all-start = ((f32[32,1,2624]{2,1,0:T(1,128)}), f32[32,1,2624]{2,1,0:T(1,128)S(1)}, u32[]{:S(2)}, u32[]{:S(2)}) async-start(f32[32,1,2624]{2,1,0:T(1,128)} %reshape.56), calls=%async_computation | async-start | bytes 688128 | tf_op jit(solution)/shard_map/all_to_all | solution.py:208

commit v2 on v1

v2 whole, which is shorter than its diff:
```python
import functools

import jax
import jax.numpy as jnp
from jax import lax
from jax.experimental import pallas as pl
from jax.experimental.pallas import tpu as pltpu
from jax.sharding import PartitionSpec as P

BF = jnp.bfloat16
F32 = jnp.float32


def round_up(value, step):
    return (value + step - 1) // step * step


def split_parts(x):
    hi = x.astype(BF)
    lo = (x - hi.astype(F32)).astype(BF)
    return hi, lo


def dot(a, b):
    return jnp.dot(a, b, preferred_element_type=F32)


def store_cat(ref, x, step):
    rows = x.shape[0]
    hi, lo = split_parts(x)
    ref[0:rows, :] = hi
    ref[step : step + rows, :] = lo
    ref[2 * step : 2 * step + rows, :] = hi


def weight_cat(ref, w, step):
    cols = w.shape[1]
    hi, lo = split_parts(w)
    ref[:, 0:cols] = hi
    ref[:, step : step + cols] = hi
    ref[:, 2 * step : 2 * step + cols] = lo


def split_state(st_ref, sp, features, feat_pad, block_rows):
    def body(r, carry):
        x = st_ref[pl.ds(r, features, stride=block_rows), :]
        if feat_pad > features:
            x = jnp.concatenate([x, jnp.zeros((feat_pad - features, x.shape[1]), F32)], axis=0)
        hi, lo = split_parts(x)
        at = pl.ds(pl.multiple_of(r * 128, 128), 128)
        sp[0:feat_pad, at] = hi
        sp[feat_pad : 2 * feat_pad, at] = lo
        return carry

    lax.fori_loop(0, block_rows, body, 0)


def build_onehot(cell, oh, at, block_rows, block_cols):
    n = cell.shape[1]
    row = jnp.floor(cell * (1.0 / block_cols))
    col = cell - row * block_cols
    lanes = lax.broadcasted_iota(jnp.int32, (block_cols, n), 0).astype(F32)
    colhot = jnp.where(lanes == col, 1.0, 0.0).astype(BF).reshape(block_cols // 16, 16, n)
    for r in range(block_rows):
        hit = jnp.broadcast_to(jnp.where(row == float(r), 1.0, 0.0), (16, n)).astype(BF)
        oh[r * block_cols : (r + 1) * block_cols, at] = (colhot * hit[None]).reshape(block_cols, n)


MESH = pl.DeviceIdType.MESH


def prepare(w1t_ref, w2_ref, wo_ref, b1_ref, b2_ref, bo_ref, coeft_ref, w1c, w1tc, w2c, w2tc, woc, wotc, side, padded, feat_pad):
    features, hid = w1t_ref.shape
    channels = wo_ref.shape[0]
    preds = coeft_ref.shape[0]
    kp = padded.shape[0]
    padded[...] = jnp.zeros_like(padded)
    padded[0:features, :] = w1t_ref[...]
    weight_cat(w1tc, padded[0:feat_pad, :], hid)
    weight_cat(w1c, padded[...].T, kp)
    w2 = w2_ref[...]
    weight_cat(w2c, w2, hid)
    weight_cat(w2tc, w2.T, hid)
    wo = wo_ref[...]
    weight_cat(woc, wo, hid)
    hi = wo.astype(BF).astype(F32)
    base = 3 * channels
    padded[...] = jnp.zeros_like(padded)
    padded[0:channels, :] = hi
    padded[channels : 2 * channels, :] = hi
    padded[2 * channels : base, :] = wo - hi
    padded[base : base + 1, :] = b1_ref[...]
    padded[base + 1 : base + 2, :] = b2_ref[...]
    padded[base + 2 : base + 3, 0:channels] = bo_ref[...]
    padded[base + 8 : base + 8 + preds, 0:channels] = coeft_ref[...]
    turned = padded[0:128, :].T
    side[...] = turned
    wotc[...] = turned.astype(BF)


def fused_kernel(
    dims, cell_ref, cnt_ref, obs_ref, wgt_ref, pred_ref, coeft_ref, st_hbm, w1t_hbm, b1_ref, w2_hbm, b2_ref, wo_ref, bo_ref,
    grad_ref, evolved_ref, bias_ref,
    w1c, w1tc, w2c, w2tc, woc, wotc, sp, oh, pcat, hcat, rcat, h1, h2, inc, res, padded, side,
    st_ref, w1t_ref, w2_ref, cell_send, cell_recv, main_send, main_recv, out_send, out_recv, bias_send, bias_recv,
    incoming, load_sem, send_sem, recv_sem,
):
    features, block_rows, block_cols, ts, nx, ny = dims
    devices = nx * ny
    hid = w2_ref.shape[0]
    channels = wo_ref.shape[0]
    half = channels // 2
    preds = coeft_ref.shape[0]
    base = 3 * channels
    feat_pad = sp.shape[0] // 2
    kp = padded.shape[0]
    slots = obs_ref.shape[1]
    cap = slots // devices
    group = 128 // cap
    me = lax.axis_index("gx") * ny + lax.axis_index("gy")

    loads = [
        pltpu.make_async_copy(src, dst, load_sem.at[k])
        for k, (src, dst) in enumerate(((st_hbm, st_ref), (w1t_hbm, w1t_ref), (w2_hbm, w2_ref)))
    ]
    for load in loads:
        load.start()

    barrier = pltpu.get_barrier_semaphore()

    def greet(k, carry):
        peer = lax.rem(me + k, devices)
        pl.semaphore_signal(barrier, inc=1, device_id=(lax.div(peer, ny), lax.rem(peer, ny)), device_id_type=MESH)
        return carry

    lax.fori_loop(1, devices, greet, 0)

    lane = lax.broadcasted_iota(jnp.int32, (channels, 128), 1)
    lane8 = lax.broadcasted_iota(jnp.int32, (8, 128), 1)

    def turn(x, shift):
        shift = shift % 128
        return pltpu.roll(x, shift, 1) if shift else x

    def pack(g, carry):
        at = pl.ds(pl.multiple_of(g * 128, 128), 128)
        obs, wgt, pred = obs_ref[:, at], wgt_ref[:, at], pred_ref[:, at]
        cell = jnp.broadcast_to(cell_ref[:, at].astype(F32), (8, 128))
        for i in range(group):
            owner = g * group + i
            off = i * cap
            count = cnt_ref[0, owner]
            masked = jnp.where(lane - 64 < count, turn(wgt, 64 - off), 0.0)
            main_send[owner, 0:channels, :] = jnp.where(lane < 64, turn(obs, -off), masked)
            main_send[owner, channels : channels + preds, :] = turn(pred, -off)
            cell_send[owner] = turn(cell, -off)[0:1]
        return carry

    lax.fori_loop(0, slots // 128, pack, 0)
    pl.semaphore_wait(barrier, devices - 1)

    def remote(src, dst, kind, peer):
        return pltpu.make_async_remote_copy(
            src_ref=src, dst_ref=dst, send_sem=send_sem.at[kind], recv_sem=recv_sem.at[kind],
            device_id=(lax.div(peer, ny), lax.rem(peer, ny)), device_id_type=MESH,
        )

    def send_cells(k, carry):
        peer = lax.rem(me + k, devices)
        remote(cell_send.at[peer], cell_recv.at[me], 0, peer).start()
        return carry

    def send_main(k, carry):
        peer = lax.rem(me + k, devices)
        remote(main_send.at[peer], main_recv.at[me], 1, peer).start()
        return carry

    lax.fori_loop(1, devices, send_cells, 0)
    lax.fori_loop(1, devices, send_main, 0)
    cell_recv[me] = cell_send[me]
    main_recv[me] = main_send[me]

    def wait_all(ref, sem):
        part = ref.at[pl.ds(0, devices - 1)]
        pltpu.make_async_copy(part, part, sem).wait()

    loads[1].wait()
    loads[2].wait()
    prepare(w1t_ref, w2_ref, wo_ref, b1_ref, b2_ref, bo_ref, coeft_ref, w1c, w1tc, w2c, w2tc, woc, wotc, side, padded, feat_pad)
    pcat[...] = jnp.zeros_like(pcat)
    rcat[...] = jnp.zeros_like(rcat)
    loads[0].wait()
    split_state(st_ref, sp, features, feat_pad, block_rows)
    wait_all(cell_recv, recv_sem.at[0])

    def chunk(t, carry):
        at = pl.ds(pl.multiple_of(t * ts, 128), ts)
        first = t * (ts // cap)
        tiles = []
        for g in range(ts // 128):
            row = jnp.zeros((8, 128), F32)
            for i in range(group):
                piece = jnp.broadcast_to(cell_recv[first + g * group + i], (8, 128))
                here = (lane8 >= i * cap) & (lane8 < (i + 1) * cap)
                row = jnp.where(here, turn(piece, i * cap), row)
            tiles.append(row)
        cell = jnp.concatenate(tiles, axis=1)[0:1]
        build_onehot(cell, oh, at, block_rows, block_cols)
        picked = dot(sp[...], oh[:, at]).astype(BF)
        pcat[0:feat_pad, :] = picked[0:feat_pad]
        pcat[kp : kp + feat_pad, :] = picked[feat_pad:]
        pcat[2 * kp : 2 * kp + feat_pad, :] = picked[0:feat_pad]
        a1 = jnp.tanh(dot(w1c[...], pcat[...]) + side[:, base : base + 1])
        h1[...] = a1
        store_cat(hcat, a1, hid)
        a2 = jnp.tanh(dot(w2c[...], hcat[...]) + side[:, base + 1 : base + 2])
        h2[...] = a2
        store_cat(hcat, a2, hid)

        @pl.when(t == 0)
        def _():
            wait_all(main_recv, recv_sem.at[1])

        for g in range(ts // 128):
            spot = slice(g * 128, (g + 1) * 128)
            value = jnp.zeros((channels, 128), F32)
            weight = jnp.zeros((channels, 128), F32)
            factor = jnp.zeros((preds, 128), F32)
            for i in range(group):
                got = main_recv[first + g * group + i]
                here = (lane >= i * cap) & (lane < (i + 1) * cap)
                value = jnp.where(here, turn(got[0:channels], i * cap), value)
                weight = jnp.where(here, turn(got[0:channels], i * cap - 64), weight)
                factor = jnp.where(here[0:preds], turn(got[channels : channels + preds], i * cap), factor)
            incoming[t, 0:channels, spot] = value
            incoming[t, channels : 2 * channels, spot] = weight
            incoming[t, 2 * channels : 2 * channels + preds, spot] = factor
        obs = incoming[t, 0:channels, :]
        wgt = incoming[t, channels : 2 * channels, :]
        pred = incoming[t, 2 * channels : 2 * channels + preds, :]
        model = dot(woc[...], hcat[...]) + side[0:channels, base + 2 : base + 3]
        for p in range(preds):
            model = model + side[0:channels, base + 8 + p : base + 9 + p] * pred[p : p + 1, :]
        residual = wgt * (model - obs)
        res[t] = residual
        for g in range(ts // 128):
            spot = slice(g * 128, (g + 1) * 128)
            upper, lower = model[0:half, spot], model[half:, spot]
            for i in range(group):
                out_send[first + g * group + i] = jnp.where(
                    lane8 < 64, turn(upper, -i * cap), turn(lower, 64 - i * cap)
                )

        def give_back(n, carry):
            peer = first + n

            @pl.when(peer != me)
            def _():
                remote(out_send.at[peer], out_recv.at[me], 2, peer).start()

            return carry

        lax.fori_loop(0, ts // cap, give_back, 0)
        store_cat(rcat, residual, channels)
        a2 = h2[...]
        store_cat(hcat, dot(wotc[...], rcat[...]) * (1.0 - a2 * a2), hid)
        a1 = h1[...]
        store_cat(hcat, dot(w2tc[...], hcat[...]) * (1.0 - a1 * a1), hid)
        hi, lo = split_parts(dot(w1tc[...], hcat[...]))
        inc[0:feat_pad, at] = hi
        inc[feat_pad : 2 * feat_pad, at] = lo
        return carry

    lax.fori_loop(0, slots // ts, chunk, 0)
    out_recv[me] = out_send[me]
    terms = jnp.zeros((preds, channels), F32)
    for t in range(slots // ts):
        terms = terms + lax.dot_general(
            incoming[t, 2 * channels : 2 * channels + preds, :], res[t], (((1,), (1,)), ((), ())),
            preferred_element_type=F32, precision=lax.Precision.HIGHEST,
        )
    bias_send[...] = jnp.zeros_like(bias_send)
    bias_send[:, 0:channels] = terms
    bias_recv[me] = bias_send[...]

    def send_bias(k, carry):
        peer = lax.rem(me + k, devices)
        remote(bias_send, bias_recv.at[me], 3, peer).start()
        return carry

    lax.fori_loop(1, devices, send_bias, 0)
    per = max(1, 256 // block_cols)

    def spread(q, carry):
        cells = pl.ds(pl.multiple_of(q * per * block_cols, 128), per * block_cols)
        got = lax.dot_general(
            inc[...], oh[cells, :], (((1,), (1,)), ((), ())), preferred_element_type=F32
        )
        total = got[0:features] + got[feat_pad : feat_pad + features]
        for k in range(per):
            grad_ref[pl.ds(q * per + k, features, stride=block_rows), :] = total[
                :, k * block_cols : (k + 1) * block_cols
            ]
        return carry

    lax.fori_loop(0, block_rows // per, spread, 0)
    wait_all(out_recv, recv_sem.at[2])

    def finish(g, carry):
        at = pl.ds(pl.multiple_of(g * 128, 128), 128)
        upper = jnp.zeros((half, 128), F32)
        lower = jnp.zeros((half, 128), F32)
        for i in range(group):
            block = g * group + i
            got = out_recv[block]
            here = (lane8 >= i * cap) & (lane8 < i * cap + jnp.minimum(cnt_ref[0, block], cap))
            upper = jnp.where(here, turn(got, i * cap), upper)
            lower = jnp.where(here, turn(got, i * cap - 64), lower)
        evolved_ref[0:half, at] = upper
        evolved_ref[half:channels, at] = lower
        return carry

    lax.fori_loop(0, slots // 128, finish, 0)
    wait_all(bias_recv, recv_sem.at[3])
    bias_ref[...] = jnp.sum(bias_recv[...], axis=0)[:, 0:channels]
    wait_all(cell_send, send_sem.at[0])
    wait_all(main_send, send_sem.at[1])
    wait_all(out_send, send_sem.at[2])
    wait_all(bias_recv, send_sem.at[3])


def per_device(
    nx, ny, model_state, obs_cell, obs_count, obs_value, obs_weight, predictor, bias_coef,
    weight_in, bias_in, weight_mid, bias_mid, weight_out, bias_out,
):
    features, block_rows, block_cols = model_state.shape
    cells = block_rows * block_cols
    hid = weight_mid.shape[0]
    channels, preds = bias_coef.shape
    slots = obs_value.shape[1]
    devices = nx * ny
    ts = min(512, slots)
    fp = round_up(features, 16)
    kp = round_up(features, 256)
    vmem = pl.BlockSpec(memory_space=pltpu.VMEM)
    hbm = pl.BlockSpec(memory_space=pl.ANY)
    smem = pl.BlockSpec(memory_space=pltpu.SMEM)
    rows = channels + preds
    gradient, evolved, bias = pl.pallas_call(
        functools.partial(fused_kernel, (features, block_rows, block_cols, ts, nx, ny)),
        out_shape=(
            jax.ShapeDtypeStruct((features * block_rows, block_cols), F32),
            jax.ShapeDtypeStruct((channels, slots), F32),
            jax.ShapeDtypeStruct((preds, channels), F32),
        ),
        in_specs=[vmem, smem, vmem, vmem, vmem, vmem, hbm, hbm, vmem, hbm, vmem, vmem, vmem],
        out_specs=(vmem,) * 3,
        scratch_shapes=[
            pltpu.VMEM((hid, 3 * kp), BF),
            pltpu.VMEM((fp, 3 * hid), BF),
            pltpu.VMEM((hid, 3 * hid), BF),
            pltpu.VMEM((hid, 3 * hid), BF),
            pltpu.VMEM((channels, 3 * hid), BF),
            pltpu.VMEM((hid, 128), BF),
            pltpu.VMEM((2 * fp, cells), BF),
            pltpu.VMEM((cells, slots), BF),
            pltpu.VMEM((3 * kp, ts), BF),
            pltpu.VMEM((3 * hid, ts), BF),
            pltpu.VMEM((128, ts), BF),
            pltpu.VMEM((hid, ts), F32),
            pltpu.VMEM((hid, ts), F32),
            pltpu.VMEM((2 * fp, slots), BF),
            pltpu.VMEM((slots // ts, channels, ts), F32),
            pltpu.VMEM((kp, hid), F32),
            pltpu.VMEM((hid, 128), F32),
            pltpu.VMEM((features * block_rows, block_cols), F32),
            pltpu.VMEM((features, hid), F32),
            pltpu.VMEM((hid, hid), F32),
            pltpu.VMEM((devices, 1, 128), F32),
            pltpu.VMEM((devices, 1, 128), F32),
            pltpu.VMEM((devices, rows, 128), F32),
            pltpu.VMEM((devices, rows, 128), F32),
            pltpu.VMEM((devices, channels // 2, 128), F32),
            pltpu.VMEM((devices, channels // 2, 128), F32),
            pltpu.VMEM((preds, 128), F32),
            pltpu.VMEM((devices, preds, 128), F32),
            pltpu.VMEM((slots // ts, 2 * channels + preds, ts), F32),
            pltpu.SemaphoreType.DMA((3,)),
            pltpu.SemaphoreType.DMA((4,)),
            pltpu.SemaphoreType.DMA((4,)),
        ],
        compiler_params=pltpu.CompilerParams(
            vmem_limit_bytes=60 * 1024 * 1024, collective_id=0, has_side_effects=True
        ),
        name="observe_all",
    )(
        obs_cell, obs_count, obs_value, obs_weight, predictor, bias_coef.T,
        model_state.reshape(features * block_rows, block_cols), weight_in.T,
        bias_in[None, :], weight_mid, bias_mid[None, :], weight_out, bias_out[None, :],
    )
    return (gradient.reshape(model_state.shape), evolved, bias.T)


def solution(mesh):
    split = ("gx", "gy")
    in_specs = (P(None, "gx", "gy"), P(split, None), P(split, None), P(None, split), P(None, split), P(None, split)) + (P(),) * 7
    out_specs = (P(None, "gx", "gy"), P(None, split), P())
    local = functools.partial(per_device, mesh.shape["gx"], mesh.shape["gy"])
    return jax.shard_map(local, mesh=mesh, in_specs=in_specs, out_specs=out_specs, check_vma=False)
```

time: 95.8 us -> 70.5 us (0.74)
  blocking collectives: 9.91 us -> 0 us
  Pallas kernels: 52.3 us -> 61.9 us
  waiting for transfers between devices: 9.32 us -> 0 us
  starting transfers between devices: 7.3 us -> 0 us
  other arithmetic: 5.52 us -> 0 us
  local copies, waits for them, and re-layouts: 10.3 us -> 7.78 us
    all_to_all x1 -> x0, blocking collectives: 9.91 us -> none  [per_device(): lax.all_to_all(back, ('gx', 'gy'), split_axis=0, concat_axis=0, tiled=True)]
    pallas_call x1, Pallas kernels: 52.3 us -> 61.9 us  [per_device(): pl.pallas_call(functools.partial(fused_kernel, (features, block_rows, blo...]
    all_to_all x1 -> x0, waiting for transfers between devices: 9.32 us -> none  [exchange_blocks(): lax.all_to_all(block_data, ('gx', 'gy'), split_axis=1, concat_axis=1, til...]
    all_to_all x1 -> x0, starting transfers between devices: 7.3 us -> none  [exchange_blocks(): lax.all_to_all(block_data, ('gx', 'gy'), split_axis=1, concat_axis=1, til...]
    all_to_all x6 -> x0, local copies, waits for them, and re-layouts: 2.53 us -> none  [the longest x5 2.37 us: exchange_blocks(): lax.all_to_all(block_data, ('gx', 'gy'), split_axis=1, concat_axis=1, til...]
    unnamed x13 -> x7, local copies, waits for them, and re-layouts: 2.73 us -> 5.25 us
    reshape x6 -> x0, local copies, waits for them, and re-layouts: 1.59 us -> none  [the longest x3 1.29 us: per_device(): local_out.reshape(channels, devices, capacity).transpose(1, 0, 2)]
    select_n x2 -> x0, other arithmetic: 1.59 us -> none  [the longest x1 0.92 us: per_device(): masked_weight = jnp.where(valid_slot[None, :], obs_weight, jnp.float32(0.0))]
  transfers between devices with their start and end apart: 1 -> 0, of which waited for: 1 -> 0; matrix products, arithmetic and copies ran while one was open for 3% -> 0% of each run, Pallas kernels for 0% -> 0%
where the time goes in v2:
time: 70.5 us; the launch traced here: 70.3 us
  Pallas kernels  61.9 us (88%)
  local copies, waits for them, and re-layouts  7.78 us (11%)
    pallas_call x1, Pallas kernels, per_device(): pl.pallas_call(functools.partial(fused_kernel, (features, block_rows, blo...  61.9 us
    unnamed x7, local copies, waits for them, and re-layouts  5.25 us

profile of v2, /device:TPU:0, one launch (start us, length us, event | category | flops | bytes accessed | tf_op | source)
XLA Modules:
  0.0 70.3 jit_solution(13707634903959508029)
XLA Ops:
  0.6 1.3 %broadcast_in_dim.9.b1_ref = f32[1,768]{1,0:T(1,128)} reshape(f32[768]{0:T(1024)} %param.21) | data formatting | bytes 6144 | tf_op jit(solution)/shard_map/broadcast_in_dim | solution.py:399
  1.9 1.3 %broadcast_in_dim.10.b2_ref = f32[1,768]{1,0:T(1,128)} reshape(f32[768]{0:T(1024)} %param.23) | data formatting | bytes 6144 | tf_op jit(solution)/shard_map/broadcast_in_dim | solution.py:399
  3.2 61.9 %observe_all.1 = (f32[6400,128]{1,0:T(8,128)}, f32[16,2048]{1,0:T(8,128)}, f32[8,16]{1,0:T(8,128)}) custom-call(s32[1,2048]{1,0:T(1,128)} %cell_ref.1, s32[1,32]{1,0:T(1,128)} %cnt_ref.1, f32[16,2048]{1,0:T(8,128)} %obs_ref.1, f32[16,2048]{1,0:T(8,128)} %wgt_ref.1, f32[8,2048]{1,0:T(8,128)} %pred_ref.1, f32[8,16]{1,0:T(8,128)} %bitcast.10, ...), custom_call_target="tpu_custom_call" | custom-call | tf_op jit(solution)/shard_map/observe_all/pallas_call | solution.py:349
  65.0 0.0 copy-start
  65.1 0.0 copy-start.1
  65.1 4.0 %copy.19 = f32[200,32,128]{2,1,0:T(8,128)} copy(f32[200,32,128]{2,1,0:T(8,128)} %bitcast.6) | data formatting | bytes 6553600
  69.1 0.0 copy-done
  69.1 0.7 copy.20
  69.7 0.0 copy-done.1
  69.7 0.6 copy.21
Async XLA Ops:
  65.0 4.0 %copy-start = (f32[16,2048]{1,0:T(8,128)S(1)}, f32[16,2048]{1,0:T(8,128)}, u32[]{:S(2)}) copy-start(f32[16,2048]{1,0:T(8,128)} %get-tuple-element.13) | copy-start | bytes 393220
  65.1 4.7 %copy-start.1 = (f32[8,16]{1,0:T(8,128)S(1)}, f32[8,16]{1,0:T(8,128)}, u32[]{:S(2)}) copy-start(f32[8,16]{1,0:T(8,128)} %get-tuple-element.8) | copy-start | bytes 1540

commit v3 on v2

--- a/solution.py
+++ b/solution.py
@@ -89,8 +89,8 @@
     padded[0:channels, :] = hi
     padded[channels : 2 * channels, :] = hi
     padded[2 * channels : base, :] = wo - hi
-    padded[base : base + 1, :] = b1_ref[...]
-    padded[base + 1 : base + 2, :] = b2_ref[...]
+    padded[base : base + 1, :] = b1_ref[...].reshape(1, hid)
+    padded[base + 1 : base + 2, :] = b2_ref[...].reshape(1, hid)
     padded[base + 2 : base + 3, 0:channels] = bo_ref[...]
     padded[base + 8 : base + 8 + preds, 0:channels] = coeft_ref[...]
     turned = padded[0:128, :].T
@@ -100,8 +100,8 @@
 
 def fused_kernel(
     dims, cell_ref, cnt_ref, obs_ref, wgt_ref, pred_ref, coeft_ref, st_hbm, w1t_hbm, b1_ref, w2_hbm, b2_ref, wo_ref, bo_ref,
-    grad_ref, evolved_ref, bias_ref,
-    w1c, w1tc, w2c, w2tc, woc, wotc, sp, oh, pcat, hcat, rcat, h1, h2, inc, res, padded, side,
+    inc, cells_ref, evolved_ref, bias_ref,
+    w1c, w1tc, w2c, w2tc, woc, wotc, sp, oh, pcats, hcats, gcats, rcats, h1s, h2s, terms_ref, padded, side,
     st_ref, w1t_ref, w2_ref, cell_send, cell_recv, main_send, main_recv, out_send, out_recv, bias_send, bias_recv,
     incoming, load_sem, send_sem, recv_sem,
 ):
@@ -145,7 +145,6 @@
     def pack(g, carry):
         at = pl.ds(pl.multiple_of(g * 128, 128), 128)
         obs, wgt, pred = obs_ref[:, at], wgt_ref[:, at], pred_ref[:, at]
-        cell = jnp.broadcast_to(cell_ref[:, at].astype(F32), (8, 128))
         for i in range(group):
             owner = g * group + i
             off = i * cap
@@ -153,10 +152,16 @@
             masked = jnp.where(lane - 64 < count, turn(wgt, 64 - off), 0.0)
             main_send[owner, 0:channels, :] = jnp.where(lane < 64, turn(obs, -off), masked)
             main_send[owner, channels : channels + preds, :] = turn(pred, -off)
-            cell_send[owner] = turn(cell, -off)[0:1]
-        return carry
-
-    lax.fori_loop(0, slots // 128, pack, 0)
+        return carry
+
+    def pack_cells(g, carry):
+        at = pl.ds(pl.multiple_of(g * 128, 128), 128)
+        cell = jnp.broadcast_to(cell_ref[:, at].astype(F32), (8, 128))
+        for i in range(group):
+            cell_send[g * group + i] = turn(cell, -i * cap)[0:1]
+        return carry
+
+    lax.fori_loop(0, slots // 128, pack_cells, 0)
     pl.semaphore_wait(barrier, devices - 1)
 
     def remote(src, dst, kind, peer):
@@ -176,6 +181,7 @@
         return carry
 
     lax.fori_loop(1, devices, send_cells, 0)
+    lax.fori_loop(0, slots // 128, pack, 0)
     lax.fori_loop(1, devices, send_main, 0)
     cell_recv[me] = cell_send[me]
     main_recv[me] = main_send[me]
@@ -187,11 +193,17 @@
     loads[1].wait()
     loads[2].wait()
     prepare(w1t_ref, w2_ref, wo_ref, b1_ref, b2_ref, bo_ref, coeft_ref, w1c, w1tc, w2c, w2tc, woc, wotc, side, padded, feat_pad)
-    pcat[...] = jnp.zeros_like(pcat)
-    rcat[...] = jnp.zeros_like(rcat)
+    pcats[...] = jnp.zeros_like(pcats)
+    rcats[...] = jnp.zeros_like(rcats)
+    terms_ref[...] = jnp.zeros_like(terms_ref)
     loads[0].wait()
     split_state(st_ref, sp, features, feat_pad, block_rows)
     wait_all(cell_recv, recv_sem.at[0])
+
+    def send_bias(k, carry):
+        peer = lax.rem(me + k, devices)
+        remote(bias_send, bias_recv.at[me], 3, peer).start()
+        return carry
 
     def chunk(t, carry):
         at = pl.ds(pl.multiple_of(t * ts, 128), ts)
@@ -205,17 +217,24 @@
                 row = jnp.where(here, turn(piece, i * cap), row)
             tiles.append(row)
         cell = jnp.concatenate(tiles, axis=1)[0:1]
-        build_onehot(cell, oh, at, block_rows, block_cols)
-        picked = dot(sp[...], oh[:, at]).astype(BF)
-        pcat[0:feat_pad, :] = picked[0:feat_pad]
-        pcat[kp : kp + feat_pad, :] = picked[feat_pad:]
-        pcat[2 * kp : 2 * kp + feat_pad, :] = picked[0:feat_pad]
-        a1 = jnp.tanh(dot(w1c[...], pcat[...]) + side[:, base : base + 1])
-        h1[...] = a1
-        store_cat(hcat, a1, hid)
-        a2 = jnp.tanh(dot(w2c[...], hcat[...]) + side[:, base + 1 : base + 2])
-        h2[...] = a2
-        store_cat(hcat, a2, hid)
+        cells_ref[:, at] = cell
+        build_onehot(cell, oh, slice(0, ts), block_rows, block_cols)
+        sub = ts // 2
+        sides = (0, 1)
+        for u in sides:
+            picked = dot(sp[...], oh[:, u * sub : (u + 1) * sub]).astype(BF)
+            pcats[u, 0:feat_pad, :] = picked[0:feat_pad]
+            pcats[u, kp : kp + feat_pad, :] = picked[feat_pad:]
+            pcats[u, 2 * kp : 2 * kp + feat_pad, :] = picked[0:feat_pad]
+        for u in sides:
+            a1 = jnp.tanh(dot(w1c[...], pcats[u]) + side[:, base : base + 1])
+            h1s[u] = a1
+            store_cat(hcats.at[u], a1, hid)
+        for u in sides:
+            a2 = jnp.tanh(dot(w2c[...], hcats[u]) + side[:, base + 1 : base + 2])
+            h2s[u] = a2
+            store_cat(gcats.at[u], a2, hid)
+        heads = [dot(woc[...], gcats[u]) for u in sides]
 
         @pl.when(t == 0)
         def _():
@@ -238,11 +257,14 @@
         obs = incoming[t, 0:channels, :]
         wgt = incoming[t, channels : 2 * channels, :]
         pred = incoming[t, 2 * channels : 2 * channels + preds, :]
-        model = dot(woc[...], hcat[...]) + side[0:channels, base + 2 : base + 3]
+        model = jnp.concatenate(heads, axis=1) + side[0:channels, base + 2 : base + 3]
         for p in range(preds):
             model = model + side[0:channels, base + 8 + p : base + 9 + p] * pred[p : p + 1, :]
         residual = wgt * (model - obs)
-        res[t] = residual
+        terms_ref[:, 0:channels] += lax.dot_general(
+            pred, residual, (((1,), (1,)), ((), ())),
+            preferred_element_type=F32, precision=lax.Precision.HIGHEST,
+        )
         for g in range(ts // 128):
             spot = slice(g * 128, (g + 1) * 128)
             upper, lower = model[0:half, spot], model[half:, spot]
@@ -261,49 +283,30 @@
             return carry
 
         lax.fori_loop(0, ts // cap, give_back, 0)
-        store_cat(rcat, residual, channels)
-        a2 = h2[...]
-        store_cat(hcat, dot(wotc[...], rcat[...]) * (1.0 - a2 * a2), hid)
-        a1 = h1[...]
-        store_cat(hcat, dot(w2tc[...], hcat[...]) * (1.0 - a1 * a1), hid)
-        hi, lo = split_parts(dot(w1tc[...], hcat[...]))
-        inc[0:feat_pad, at] = hi
-        inc[feat_pad : 2 * feat_pad, at] = lo
+
+        @pl.when(t == slots // ts - 1)
+        def _():
+            bias_send[...] = terms_ref[...]
+            lax.fori_loop(1, devices, send_bias, 0)
+
+        for u in sides:
+            store_cat(rcats.at[u], residual[:, u * sub : (u + 1) * sub], channels)
+        for u in sides:
+            a2 = h2s[u]
+            store_cat(hcats.at[u], dot(wotc[...], rcats[u]) * (1.0 - a2 * a2), hid)
+        for u in sides:
+            a1 = h1s[u]
+            store_cat(gcats.at[u], dot(w2tc[...], hcats[u]) * (1.0 - a1 * a1), hid)
+        for u in sides:
+            hi, lo = split_parts(dot(w1tc[...], gcats[u]))
+            here = pl.ds(pl.multiple_of(t * ts + u * sub, 128), sub)
+            inc[0:feat_pad, here] = hi
+            inc[feat_pad : 2 * feat_pad, here] = lo
         return carry
 
     lax.fori_loop(0, slots // ts, chunk, 0)
     out_recv[me] = out_send[me]
-    terms = jnp.zeros((preds, channels), F32)
-    for t in range(slots // ts):
-        terms = terms + lax.dot_general(
-            incoming[t, 2 * channels : 2 * channels + preds, :], res[t], (((1,), (1,)), ((), ())),
-            preferred_element_type=F32, precision=lax.Precision.HIGHEST,
-        )
-    bias_send[...] = jnp.zeros_like(bias_send)
-    bias_send[:, 0:channels] = terms
     bias_recv[me] = bias_send[...]
-
-    def send_bias(k, carry):
-        peer = lax.rem(me + k, devices)
-        remote(bias_send, bias_recv.at[me], 3, peer).start()
-        return carry
-
-    lax.fori_loop(1, devices, send_bias, 0)
-    per = max(1, 256 // block_cols)
-
-    def spread(q, carry):
-        cells = pl.ds(pl.multiple_of(q * per * block_cols, 128), per * block_cols)
-        got = lax.dot_general(
-            inc[...], oh[cells, :], (((1,), (1,)), ((), ())), preferred_element_type=F32
-        )
-        total = got[0:features] + got[feat_pad : feat_pad + features]
-        for k in range(per):
-            grad_ref[pl.ds(q * per + k, features, stride=block_rows), :] = total[
-                :, k * block_cols : (k + 1) * block_cols
-            ]
-        return carry
-
-    lax.fori_loop(0, block_rows // per, spread, 0)
     wait_all(out_recv, recv_sem.at[2])
 
     def finish(g, carry):
@@ -327,6 +330,36 @@
     wait_all(main_send, send_sem.at[1])
     wait_all(out_send, send_sem.at[2])
     wait_all(bias_recv, send_sem.at[3])
+
+
+def spread_kernel(inc_ref, cells_ref, grad_ref, colhot, oh):
+    features, row_step, block_cols = grad_ref.shape
+    feat_pad = inc_ref.shape[0] // 2
+    n = inc_ref.shape[1]
+    step = pl.program_id(0)
+    cell = cells_ref[...]
+    row = jnp.floor(cell * (1.0 / block_cols))
+
+    @pl.when(step == 0)
+    def _():
+        lanes = lax.broadcasted_iota(jnp.int32, (block_cols, n), 0).astype(F32)
+        colhot[...] = jnp.where(lanes == cell - row * block_cols, 1.0, 0.0).astype(BF)
+
+    away = row - (step * row_step).astype(F32)
+    per = max(1, 256 // block_cols)
+    for q in range(row_step // per):
+        for k in range(per):
+            hit = jnp.where(away == float(q * per + k), 1.0, 0.0)
+            hit = jnp.broadcast_to(hit, (16, n)).astype(BF)
+            part = colhot[...].reshape(block_cols // 16, 16, n) * hit[None]
+            oh[q, k * block_cols : (k + 1) * block_cols, :] = part.reshape(block_cols, n)
+    for q in range(row_step // per):
+        got = lax.dot_general(
+            inc_ref[...], oh[q], (((1,), (1,)), ((), ())), preferred_element_type=F32
+        )
+        total = got[0:features] + got[feat_pad : feat_pad + features]
+        for k in range(per):
+            grad_ref[:, q * per + k, :] = total[:, k * block_cols : (k + 1) * block_cols]
 
 
 def per_device(
@@ -346,15 +379,16 @@
     hbm = pl.BlockSpec(memory_space=pl.ANY)
     smem = pl.BlockSpec(memory_space=pltpu.SMEM)
     rows = channels + preds
-    gradient, evolved, bias = pl.pallas_call(
+    parts, chosen, evolved, bias = pl.pallas_call(
         functools.partial(fused_kernel, (features, block_rows, block_cols, ts, nx, ny)),
         out_shape=(
-            jax.ShapeDtypeStruct((features * block_rows, block_cols), F32),
+            jax.ShapeDtypeStruct((2 * fp, slots), BF),
+            jax.ShapeDtypeStruct((1, slots), F32),
             jax.ShapeDtypeStruct((channels, slots), F32),
             jax.ShapeDtypeStruct((preds, channels), F32),
         ),
         in_specs=[vmem, smem, vmem, vmem, vmem, vmem, hbm, hbm, vmem, hbm, vmem, vmem, vmem],
-        out_specs=(vmem,) * 3,
+        out_specs=(vmem,) * 4,
         scratch_shapes=[
             pltpu.VMEM((hid, 3 * kp), BF),
             pltpu.VMEM((fp, 3 * hid), BF),
@@ -363,14 +397,14 @@
             pltpu.VMEM((channels, 3 * hid), BF),
             pltpu.VMEM((hid, 128), BF),
             pltpu.VMEM((2 * fp, cells), BF),
-            pltpu.VMEM((cells, slots), BF),
-            pltpu.VMEM((3 * kp, ts), BF),
-            pltpu.VMEM((3 * hid, ts), BF),
-            pltpu.VMEM((128, ts), BF),
-            pltpu.VMEM((hid, ts), F32),
-            pltpu.VMEM((hid, ts), F32),
-            pltpu.VMEM((2 * fp, slots), BF),
-            pltpu.VMEM((slots // ts, channels, ts), F32),
+            pltpu.VMEM((cells, ts), BF),
+            pltpu.VMEM((2, 3 * kp, ts // 2), BF),
+            pltpu.VMEM((2, 3 * hid, ts // 2), BF),
+            pltpu.VMEM((2, 3 * hid, ts // 2), BF),
+            pltpu.VMEM((2, 128, ts // 2), BF),
+            pltpu.VMEM((2, hid, ts // 2), F32),
+            pltpu.VMEM((2, hid, ts // 2), F32),
+            pltpu.VMEM((preds, 128), F32),
             pltpu.VMEM((kp, hid), F32),
             pltpu.VMEM((hid, 128), F32),
             pltpu.VMEM((features * block_rows, block_cols), F32),
@@ -396,9 +430,23 @@
     )(
         obs_cell, obs_count, obs_value, obs_weight, predictor, bias_coef.T,
         model_state.reshape(features * block_rows, block_cols), weight_in.T,
-        bias_in[None, :], weight_mid, bias_mid[None, :], weight_out, bias_out[None, :],
+        bias_in, weight_mid, bias_mid, weight_out, bias_out[None, :],
     )
-    return (gradient.reshape(model_state.shape), evolved, bias.T)
+    row_step = min(8, block_rows)
+    gradient = pl.pallas_call(
+        spread_kernel,
+        grid=(block_rows // row_step,),
+        out_shape=jax.ShapeDtypeStruct(model_state.shape, F32),
+        in_specs=[vmem, vmem],
+        out_specs=pl.BlockSpec((features, row_step, block_cols), lambda g: (0, g, 0)),
+        scratch_shapes=[
+            pltpu.VMEM((block_cols, slots), BF),
+            pltpu.VMEM((row_step * block_cols // 256, 256, slots), BF),
+        ],
+        compiler_params=pltpu.CompilerParams(vmem_limit_bytes=48 * 1024 * 1024),
+        name="spread_increments",
+    )(parts, chosen)
+    return (gradient, evolved, bias.T)
 
 
 def solution(mesh):

time: 70.5 us -> 67.1 us (0.952)
  local copies, waits for them, and re-layouts: 7.78 us -> 3.4 us
  Pallas kernels: 61.9 us -> 62.8 us
    pallas_call x0 -> x1, Pallas kernels: none -> 10.4 us  [per_device(): pl.pallas_call(spread_kernel, grid=(block_rows // row_step,), out_shape=j...]
    pallas_call x1, Pallas kernels: 61.9 us -> 52.5 us  [per_device(): pl.pallas_call(functools.partial(fused_kernel, (features, block_rows, blo...]
    broadcast_in_dim x2 -> x0, local copies, waits for them, and re-layouts: 2.53 us -> none  [the longest x1 1.27 us: per_device(): bias_in[None, :]]
    unnamed x7 -> x10, local copies, waits for them, and re-layouts: 5.25 us -> 3.4 us
where the time goes in v3:
time: 67.1 us; the launch traced here: 66.9 us
  Pallas kernels  62.8 us (94%)
  local copies, waits for them, and re-layouts  3.4 us (5%)
    pallas_call x1, Pallas kernels, per_device(): pl.pallas_call(functools.partial(fused_kernel, (features, block_rows, blo...  52.5 us
    pallas_call x1, Pallas kernels, per_device(): pl.pallas_call(spread_kernel, grid=(block_rows // row_step,), out_shape=j...  10.4 us
    unnamed x10, local copies, waits for them, and re-layouts  3.4 us

profile of v3, /device:TPU:0, one launch (start us, length us, event | category | flops | bytes accessed | tf_op | source)
XLA Modules:
  0.0 66.9 jit_solution(9850038659197996407)
XLA Ops:
  0.6 52.5 %observe_all.1 = (bf16[416,2048]{1,0:T(8,128)(2,1)}, f32[1,2048]{1,0:T(1,128)}, f32[16,2048]{1,0:T(8,128)}, f32[8,16]{1,0:T(8,128)}) custom-call(s32[1,2048]{1,0:T(1,128)} %cell_ref.1, s32[1,32]{1,0:T(1,128)} %cnt_ref.1, f32[16,2048]{1,0:T(8,128)} %obs_ref.1, f32[16,2048]{1,0:T(8,128)} %wgt_ref.1, f32[8,2048]{1,0:T(8,128)} %pred_ref.1, f32[8,16]{1,0:T(8,128)} %bitcast.7, ...), custom_call_target="tpu_custom_call" | custom-call | tf_op jit(solution)/shard_map/observe_all/pallas_call | solution.py:382
  53.1 0.0 copy-start.3
  53.1 0.0 copy-start
  53.1 1.4 %copy-done = bf16[416,2048]{1,0:T(8,128)(2,1)S(1)} copy-done((bf16[416,2048]{1,0:T(8,128)(2,1)S(1)}, bf16[416,2048]{1,0:T(8,128)(2,1)}, u32[]{:S(2)}) %copy-start) | copy-done | bytes 1703960
  54.6 0.0 copy-start.1
  54.6 0.7 %copy-done.1 = f32[1,2048]{1,0:T(1,128)S(1)} copy-done((f32[1,2048]{1,0:T(1,128)S(1)}, f32[1,2048]{1,0:T(1,128)}, u32[]{:S(2)}) %copy-start.1) | copy-done | bytes 8216
  55.3 0.0 copy-start.2
  55.3 10.4 %spread_increments.1 = f32[200,32,128]{2,1,0:T(8,128)} custom-call(bf16[416,2048]{1,0:T(8,128)(2,1)S(1)} %copy-done, f32[1,2048]{1,0:T(1,128)S(1)} %copy-done.1), custom_call_target="tpu_custom_call" | custom-call | tf_op jit(solution)/shard_map/spread_increments/pallas_call | solution.py:436
  65.6 0.0 copy-done.2
  65.6 0.7 copy.18
  66.3 0.0 copy-done.3
  66.3 0.6 copy.19
Async XLA Ops:
  53.1 13.2 %copy-start.3 = (f32[8,16]{1,0:T(8,128)S(1)}, f32[8,16]{1,0:T(8,128)}, u32[]{:S(2)}) copy-start(f32[8,16]{1,0:T(8,128)} %get-tuple-element.10) | copy-start | bytes 1540
  53.1 1.5 %copy-start = (bf16[416,2048]{1,0:T(8,128)(2,1)S(1)}, bf16[416,2048]{1,0:T(8,128)(2,1)}, u32[]{:S(2)}) copy-start(bf16[416,2048]{1,0:T(8,128)(2,1)} %get-tuple-element.7.inc_ref) | copy-start | bytes 5111812
  54.6 0.7 %copy-start.1 = (f32[1,2048]{1,0:T(1,128)S(1)}, f32[1,2048]{1,0:T(1,128)}, u32[]{:S(2)}) copy-start(f32[1,2048]{1,0:T(1,128)} %get-tuple-element.8.cells_ref) | copy-start | bytes 24580
  55.3 10.4 %copy-start.2 = (f32[16,2048]{1,0:T(8,128)S(1)}, f32[16,2048]{1,0:T(8,128)}, u32[]{:S(2)}) copy-start(f32[16,2048]{1,0:T(8,128)} %get-tuple-element.15) | copy-start | bytes 393220
